TPU v7x, 32 devices: a whole 2x2x4 slice. The times are simulated.
32 devices in a mesh: dp: 8 (over z, x), tensor: 4 (over y, core).
Axes of the slice: x: 2, y: 2, z: 4, core: 2. Of those that a mesh axis runs over, the one named last changes fastest.
Arguments:
- tokens: bfloat16 [17344, 768], P(('dp', 'tensor')), may hold values from -16 to 16
- lengths: int32 [32, 6], P(('dp', 'tensor')), may hold values from 1 to 197, 542 in all within a row
- capacity: int32 [17344], P(('dp', 'tensor')), may hold values from 0 to 1, as said below
- norm1_gain: float32 [768], replicated, may hold values from 0.1 to 1.9
- router: float32 [768], replicated, may hold values from -0.21875 to 0.21875
- w_qkv: bfloat16 [768, 2304], replicated, may hold values from -0.21875 to 0.21875
- w_out: bfloat16 [768, 768], replicated, may hold values from -1.25 to 1.25
- norm2_gain: float32 [768], replicated, may hold values from 0.1 to 1.9
- w_up: bfloat16 [768, 3072], P(None, 'tensor'), may hold values from -0.21875 to 0.21875
- w_down: bfloat16 [3072, 768], P('tensor'), may hold values from -0.109375 to 0.109375
- cotangent: bfloat16 [17344, 768], P(('dp', 'tensor')), may hold values from -6 to 6
Outputs:
- mixed: bfloat16 [17344, 768], P(('dp', 'tensor'))
- grad_input: float32 [17344, 768], P(('dp', 'tensor'))
- grad_norm1_gain: float32 [768], replicated
- grad_router: float32 [768], replicated
- grad_qkv: float32 [768, 2304], P(('dp', 'tensor'))
- grad_out_proj: float32 [768, 768], P(('dp', 'tensor'))
- grad_norm2_gain: float32 [768], replicated
- grad_up: float32 [768, 3072], P(None, 'tensor')
- grad_down: float32 [3072, 768], P('tensor')
- norms: float32 [3], replicated
Inputs may be any that keep to these rules, and one draw needn't show every extreme that they name: Each image's 6 crop lengths sum to 542, and its longest crop has 197 tokens. `capacity`: exactly 271 tokens of each image are 1.
All inputs are finite; a program needn't handle non-finite values.
Results may differ from a plain program's by a relative error of at most 0.013.
Values may be sent and summed in bfloat16 or wider, within the bound.
No kernel may reach another device: no remote copies, remote signals or barrier semaphores. Data moves between devices by JAX's collectives and lax.ppermute only.
A program may use at most 192 MiB of HBM per device.

v0:
```python
import math

import jax
import jax.numpy as jnp
from jax import lax
from jax.sharding import PartitionSpec as P

HEADS = 12
HEAD_DIM = 64


EPSILON = 1e-06
NEGATIVE = -1000000000.0
HIGHEST = lax.Precision.HIGHEST
CONTRACT_ROWS = (((0,), (0,)), ((), ()))
CONTRACT_COLS = (((1,), (1,)), ((), ()))


def normalize(inputs, gain_vec):
    center = inputs - jnp.mean(inputs, axis=-1, keepdims=True)
    inverse = lax.rsqrt(jnp.mean(center * center, axis=-1, keepdims=True) + EPSILON)
    normed = center * inverse
    return (normed * gain_vec, normed, inverse)


def normalize_back(grad_out, normed, inverse, gain_vec):
    scaled = grad_out * gain_vec
    mean_grad = jnp.mean(scaled, axis=-1, keepdims=True)
    mean_cross = jnp.mean(scaled * normed, axis=-1, keepdims=True)
    return (
        inverse * (scaled - mean_grad - normed * mean_cross),
        jnp.sum(grad_out * normed, axis=0),
    )


def crop_ids(lengths, img_rows):
    crop_ends = jnp.cumsum(lengths, axis=-1)
    position = lax.broadcasted_iota(jnp.int32, (lengths.shape[0], img_rows, lengths.shape[1]), 1)
    return jnp.sum((position >= crop_ends[:, None, :]).astype(jnp.int32), axis=-1)


def allowed_keys(crop_of, chosen):
    tok_count = crop_of.shape[0]
    same_crop = crop_of[:, None] == crop_of[None, :]
    itself = lax.broadcasted_iota(jnp.int32, (tok_count, tok_count), 0) == lax.broadcasted_iota(
        jnp.int32, (tok_count, tok_count), 1
    )
    return same_crop & ((chosen[None, :] == 1) | itself)


def split_heads(united_qkv):
    tok_count = united_qkv.shape[0]
    feat_width = HEADS * HEAD_DIM
    queries = united_qkv[:, :feat_width].reshape(tok_count, HEADS, HEAD_DIM)
    key_heads = united_qkv[:, feat_width : 2 * feat_width].reshape(tok_count, HEADS, HEAD_DIM)
    values = united_qkv[:, 2 * feat_width :].reshape(tok_count, HEADS, HEAD_DIM)
    return (queries, key_heads, values)


def masked_scores(queries, key_heads, allowed):
    score_scale = 1.0 / math.sqrt(HEAD_DIM)
    raw_scores = (
        jnp.einsum("qhd,khd->hqk", queries, key_heads, preferred_element_type=jnp.float32)
        * score_scale
    )
    return jnp.where(allowed[None], raw_scores, NEGATIVE)


def attend_image(packed):
    united_qkv, crop_of, chosen = packed
    queries, key_heads, values = split_heads(united_qkv)
    scores = masked_scores(queries, key_heads, allowed_keys(crop_of, chosen))
    row_max = jnp.max(scores, axis=-1, keepdims=True)
    exponent = jnp.exp(scores - row_max)
    row_total = jnp.sum(exponent, axis=-1, keepdims=True)
    attn_prob = (exponent / row_total).astype(jnp.bfloat16)
    mixed_heads = jnp.einsum("hqk,khd->qhd", attn_prob, values, preferred_element_type=jnp.float32)
    return (
        mixed_heads.reshape(united_qkv.shape[0], -1).astype(jnp.bfloat16),
        (row_max + jnp.log(row_total))[..., 0],
    )


def attend_back(packed):
    united_qkv, crop_of, chosen, log_total, grad_mixed = packed
    tok_count = united_qkv.shape[0]
    queries, key_heads, values = split_heads(united_qkv)
    scores = masked_scores(queries, key_heads, allowed_keys(crop_of, chosen))
    attn_prob = jnp.exp(scores - log_total[..., None])
    grad_heads = grad_mixed.reshape(tok_count, HEADS, HEAD_DIM)
    grad_values = jnp.einsum(
        "hqk,qhd->khd",
        attn_prob.astype(jnp.bfloat16),
        grad_heads,
        preferred_element_type=jnp.float32,
    )
    grad_prob = jnp.einsum("qhd,khd->hqk", grad_heads, values, preferred_element_type=jnp.float32)
    grad_scores = (
        attn_prob * (grad_prob - jnp.sum(attn_prob * grad_prob, axis=-1, keepdims=True))
    ).astype(jnp.bfloat16)
    score_scale = 1.0 / math.sqrt(HEAD_DIM)
    grad_queries = (
        jnp.einsum("hqk,khd->qhd", grad_scores, key_heads, preferred_element_type=jnp.float32)
        * score_scale
    )
    grad_keys = (
        jnp.einsum("hqk,qhd->khd", grad_scores, queries, preferred_element_type=jnp.float32)
        * score_scale
    )
    joined = jnp.concatenate(
        [
            grad_queries.reshape(tok_count, -1),
            grad_keys.reshape(tok_count, -1),
            grad_values.reshape(tok_count, -1),
        ],
        axis=-1,
    )
    return joined.astype(jnp.bfloat16)


def gelu_back(pre_act, grad_act):
    unused_value, pullback = jax.vjp(
        lambda pre_value: jax.nn.gelu(pre_value, approximate=True), pre_act
    )
    return pullback(grad_act)[0]


def shards(
    tokens, lengths, capacity, norm1_gain, router, w_qkv, w_out, norm2_gain, w_up, w_down, cotangent
):
    row_count = tokens.shape[0]
    feat_width = tokens.shape[1]
    image_count = lengths.shape[0]
    img_rows = row_count // image_count
    inputs = tokens.astype(jnp.float32)
    crop_of = crop_ids(lengths, img_rows)
    chosen = capacity.reshape(image_count, img_rows)
    keep_mask = capacity.astype(jnp.float32)[:, None]
    normed1, unit_one, inverse_one = normalize(inputs, norm1_gain)
    low_one = normed1.astype(jnp.bfloat16)
    router_logit = jnp.dot(low_one, router, precision=HIGHEST, preferred_element_type=jnp.float32)
    router_gate = jax.nn.sigmoid(router_logit)[:, None]
    united_qkv = jnp.dot(low_one, w_qkv, preferred_element_type=jnp.float32).astype(jnp.bfloat16)
    united_images = united_qkv.reshape(image_count, img_rows, -1)
    mixed_heads, log_total = lax.map(attend_image, (united_images, crop_of, chosen))
    mixed_heads = mixed_heads.reshape(row_count, feat_width)
    attended = jnp.dot(mixed_heads, w_out, preferred_element_type=jnp.float32)
    branch = keep_mask * router_gate * attended
    resid = inputs + branch
    normed2, unit_two, inverse_two = normalize(resid, norm2_gain)
    low_two = normed2.astype(jnp.bfloat16)
    gathered = lax.all_gather(low_two, "tensor", axis=0, tiled=True)
    pre_act = jnp.dot(gathered, w_up, preferred_element_type=jnp.float32)
    activation = jax.nn.gelu(pre_act, approximate=True).astype(jnp.bfloat16)
    hidden_branch = lax.psum_scatter(
        jnp.dot(activation, w_down, preferred_element_type=jnp.float32).astype(jnp.bfloat16),
        "tensor",
        scatter_dimension=0,
        tiled=True,
    ).astype(jnp.float32)
    mixed = (resid + hidden_branch).astype(jnp.bfloat16)
    squares = jnp.stack(
        [jnp.sum(resid * resid), jnp.sum(branch * branch), jnp.sum(hidden_branch * hidden_branch)]
    )
    totals = lax.psum(squares, ("dp", "tensor"))
    grad_rows = lax.all_gather(cotangent, "tensor", axis=0, tiled=True)
    grad_act = lax.dot_general(grad_rows, w_down, CONTRACT_COLS, preferred_element_type=jnp.float32)
    grad_pre = gelu_back(pre_act, grad_act).astype(jnp.bfloat16)
    grad_down = lax.dot_general(
        activation, grad_rows, CONTRACT_ROWS, preferred_element_type=jnp.float32
    )
    grad_up = lax.dot_general(gathered, grad_pre, CONTRACT_ROWS, preferred_element_type=jnp.float32)
    grad_norm2 = lax.psum_scatter(
        lax.dot_general(grad_pre, w_up, CONTRACT_COLS, preferred_element_type=jnp.float32).astype(
            jnp.bfloat16
        ),
        "tensor",
        scatter_dimension=0,
        tiled=True,
    ).astype(jnp.float32)
    grad_up, grad_down = (
        lax.psum(grad_up.astype(jnp.bfloat16), "dp").astype(jnp.float32),
        lax.psum(grad_down.astype(jnp.bfloat16), "dp").astype(jnp.float32),
    )
    resid_from_norm, grad_gain_two = normalize_back(grad_norm2, unit_two, inverse_two, norm2_gain)
    grad_resid = cotangent.astype(jnp.float32) + resid_from_norm
    grad_attended = (grad_resid * keep_mask * router_gate).astype(jnp.bfloat16)
    grad_gate = jnp.sum(grad_resid * keep_mask * attended, axis=-1)
    grad_logit = grad_gate * router_gate[:, 0] * (1.0 - router_gate[:, 0])
    grad_proj = lax.dot_general(
        mixed_heads, grad_attended, CONTRACT_ROWS, preferred_element_type=jnp.float32
    )
    grad_mixed = lax.dot_general(
        grad_attended, w_out, CONTRACT_COLS, preferred_element_type=jnp.float32
    ).astype(jnp.bfloat16)
    grad_united = lax.map(
        attend_back,
        (
            united_images,
            crop_of,
            chosen,
            log_total,
            grad_mixed.reshape(image_count, img_rows, feat_width),
        ),
    )
    grad_united = grad_united.reshape(row_count, -1)
    grad_qkv = lax.dot_general(
        low_one, grad_united, CONTRACT_ROWS, preferred_element_type=jnp.float32
    )
    grad_norm1 = (
        lax.dot_general(grad_united, w_qkv, CONTRACT_COLS, preferred_element_type=jnp.float32)
        + grad_logit[:, None] * router[None, :]
    )
    grad_router = jnp.dot(
        grad_logit, low_one, precision=HIGHEST, preferred_element_type=jnp.float32
    )
    input_from_norm, grad_gain_one = normalize_back(grad_norm1, unit_one, inverse_one, norm1_gain)
    grad_input = grad_resid + input_from_norm
    qkv_share, proj_share = (
        lax.psum_scatter(grad_qkv, ("dp", "tensor"), scatter_dimension=0, tiled=True),
        lax.psum_scatter(grad_proj, ("dp", "tensor"), scatter_dimension=0, tiled=True),
    )
    shared = lax.psum((grad_gain_one, grad_router, grad_gain_two), ("dp", "tensor"))
    element_count = row_count * feat_width * lax.axis_size("dp") * lax.axis_size("tensor")
    norms = jnp.sqrt(totals / element_count)
    return (
        mixed,
        grad_input,
        shared[0],
        shared[1],
        qkv_share,
        proj_share,
        shared[2],
        grad_up,
        grad_down,
        norms,
    )


def solution(mesh):
    return jax.shard_map(
        shards,
        mesh=mesh,
        in_specs=(
            P(("dp", "tensor"), None),
            P(("dp", "tensor"), None),
            P(("dp", "tensor")),
            P(),
            P(),
            P(),
            P(),
            P(),
            P(None, "tensor"),
            P("tensor", None),
            P(("dp", "tensor"), None),
        ),
        out_specs=(
            P(("dp", "tensor"), None),
            P(("dp", "tensor"), None),
            P(),
            P(),
            P(("dp", "tensor"), None),
            P(("dp", "tensor"), None),
            P(),
            P(None, "tensor"),
            P("tensor", None),
            P(),
        ),
        check_vma=False,
    )
```

profile of v0, /device:TPU:0, one launch (start us, length us, event | category | flops | bytes accessed | tf_op | source)
XLA Modules:
  0.0 474.4 jit_solution(5166826816431138379)
XLA Ops:
  28.8 10.0 %fusion.57 = (f32[12,542]{1,0:T(8,128)S(1)}, f32[12,542,542]{1,2,0:T(8,128)}) fusion(bf16[542,12,64]{0,2,1:T(8,128)(2,1)} %bitcast.63, bf16[542,12,64]{0,2,1:T(8,128)(2,1)} %bitcast.61, pred[542,542]{0,1:T(8,128)(4,1)S(1)} %fusion.44), kind=kOutput, calls=%fused_computation.102 | convolution fusion | flops 461790528 | bytes 16085476 | tf_op jit(solution)/shard_map/while/body/eval_jaxpr/qhd,khd->hqk/dot_general | solution.py:63
  38.8 8.2 %fusion.2 = f32[12,542]{1,0:T(8,128)S(1)} fusion(f32[12,542,542]{1,2,0:T(8,128)} %get-tuple-element.79, f32[12,542]{1,0:T(8,128)S(1)} %get-tuple-element.78), kind=kLoop, calls=%fused_computation.6 | loop fusion | flops 7043832 | bytes 14152704 | tf_op jit(solution)/shard_map/while/body/eval_jaxpr/reduce_sum | solution.py:75
  47.1 9.0 %fusion.38 = bf16[12,64,542]{2,1,0:T(8,128)(2,1)S(1)} fusion(bf16[542,12,64]{0,2,1:T(8,128)(2,1)S(1)} %bitcast.70, f32[12,542,542]{1,2,0:T(8,128)} %get-tuple-element.79, f32[12,542]{1,0:T(8,128)S(1)} %fusion.2, f32[12,542]{1,0:T(8,128)S(1)} %get-tuple-element.78), kind=kOutput, calls=%fused_computation.67 | convolution fusion | flops 462213248 | bytes 15817728 | tf_op jit(solution)/shard_map/while/body/eval_jaxpr/hqk,khd->qhd/dot_general | solution.py:77
  60.9 4.6 reshape.245
  65.5 7.9 %fusion.58 = f32[2168,768]{1,0:T(8,128)} fusion(bf16[2168,768]{1,0:T(8,128)(2,1)} %reshape.245, bf16[768,768]{1,0:T(8,128)(2,1)} %param.20), kind=kOutput, calls=%fused_computation.103 | convolution fusion | flops 2557476864 | bytes 11169792 | tf_op jit(solution)/shard_map/dot_general | solution.py:167
  73.4 19.7 %all-gather.5.cloned.1.call-done = bf16[4,542,768]{2,1,0:T(8,128)(2,1)} async-done(((bf16[1,542,768]{2,1,0:T(8,128)(2,1)}), bf16[4,542,768]{2,1,0:T(8,128)(2,1)}) %all-gather.5.cloned.1.call-update) | async-done | bytes 3330064 | tf_op jit(solution)/shard_map/all_gather | solution.py:152
  93.2 4.5 reshape.243
  97.7 9.2 %fusion.14 = (bf16[2168,768]{1,0:T(8,128)(2,1)S(1)}, f32[2168,768]{1,0:T(8,128)S(1)}) fusion(f32[2168,768]{1,0:T(8,128)} %fusion.58, bf16[2168,768]{1,0:T(8,128)(2,1)} %reshape.243, bf16[768,768]{1,0:T(8,128)(2,1)} %param.19), kind=kOutput, calls=%fused_computation.19 | convolution fusion | flops 2590777344 | bytes 21159936 | tf_op jit(solution)/shard_map/dot_general | solution.py:153
  110.9 4.7 convolution_convert_fusion
  115.6 4.7 convolution_convert_fusion.3
  120.3 9.0 %convolution_convert_fusion.1 = bf16[2168,768]{1,0:T(8,128)(2,1)} fusion(bf16[768,768]{1,0:T(8,128)(2,1)} %param.20, f32[2168,768]{1,0:T(8,128)} %copy-done.37), kind=kOutput, calls=%fused_computation.22 | convolution fusion | flops 2574127104 | bytes 11169792 | tf_op jit(solution)/shard_map/dot_general | solution.py:156
  129.4 61.1 %fusion.53 = (bf16[544,768]{1,0:T(8,128)(2,1)}, bf16[544,768]{1,0:T(8,128)(2,1)}) fusion(bf16[2168,768]{1,0:T(8,128)(2,1)} %convolution_convert_fusion.1, bf16[2168,768]{1,0:T(8,128)(2,1)} %convolution_convert_fusion), kind=kCustom, calls=%all-reduce-scatter.2 | all-reduce-scatter fusion | flops 3342337 | bytes 8331776
  202.7 6.9 %concatenate.6 = bf16[550,768]{1,0:T(8,128)(2,1)} concatenate(bf16[6,768]{1,0:T(8,128)(2,1)} %collective-permute-done, bf16[544,768]{1,0:T(8,128)(2,1)} %get-tuple-element.66), dimensions={0} | concatenate | bytes 1689600
  209.5 6.7 %concatenate.7 = bf16[550,768]{1,0:T(8,128)(2,1)} concatenate(bf16[6,768]{1,0:T(8,128)(2,1)} %collective-permute-done.1, bf16[544,768]{1,0:T(8,128)(2,1)} %get-tuple-element.67), dimensions={0} | concatenate | bytes 1689600
  219.8 5.2 %multiply_reduce_fusion.1 = (f32[]{:T(128)}, f32[542]{0:T(1024)S(1)}, f32[542,768]{1,0:T(8,128)S(1)}, bf16[542,768]{1,0:T(8,128)(2,1)}, f32[]{:T(128)}) fusion(f32[542,768]{1,0:T(8,128)} %get-tuple-element.80, f32[542]{0:T(1024)} %copy-done.25, f32[542]{0:T(1024)} %convert_element_type.93, f32[542]{0:T(1024)S(1)} %get-tuple-element.86, ...), kind=kLoop, calls=%fused_computation.57 | loop fusion | flops 8740832 | bytes 8343380 | tf_op jit(solution)/shard_map/reduce_sum | solution.py:163
  230.1 4.4 fusion.52
  234.6 15.4 %multiply_reduce_fusion = (f32[12,542]{1,0:T(8,128)S(1)}, f32[12,542,542]{1,2,0:T(8,128)}) fusion(f32[12,542,542]{1,2,0:T(8,128)} %get-tuple-element.79, f32[12,542]{1,0:T(8,128)} %log_add_fusion, bf16[542,12,64]{0,2,1:T(8,128)(2,1)} %bitcast.65, bf16[542,12,64]{0,2,1:T(8,128)(2,1)} %bitcast.69), kind=kOutput, calls=%fused_computation.1 | convolution fusion | flops 461790528 | bytes 29918400 | tf_op jit(solution)/shard_map/while/body/eval_jaxpr/qhd,khd->hqk/dot_general | solution.py:97
  250.1 12.3 %multiply_convert_fusion = bf16[12,542,542]{1,2,0:T(8,128)(2,1)S(1)} fusion(f32[12,542,542]{1,2,0:T(8,128)} %get-tuple-element.84, f32[12,542,542]{1,2,0:T(8,128)} %get-tuple-element.79, f32[12,542]{1,0:T(8,128)S(1)} %get-tuple-element.83, f32[12,542]{1,0:T(8,128)S(1)} %copy-done.21), kind=kLoop, calls=%fused_computation | loop fusion | flops 14100672 | bytes 35303712 | tf_op jit(solution)/shard_map/while/body/eval_jaxpr/convert_element_type | solution.py:100
  266.9 9.1 %fusion.39 = bf16[12,64,542]{2,1,0:T(8,128)(2,1)S(1)} fusion(bf16[542,12,64]{0,2,1:T(8,128)(2,1)S(1)} %bitcast.66, f32[12,542,542]{1,2,0:T(8,128)} %get-tuple-element.79, f32[12,542]{1,0:T(8,128)S(1)} %copy-done.21), kind=kOutput, calls=%fused_computation.68 | convolution fusion | flops 458688096 | bytes 15791712 | tf_op jit(solution)/shard_map/while/body/eval_jaxpr/hqk,qhd->khd/dot_general | solution.py:91
  277.0 7.4 %fusion.45 = f32[768,2304]{1,0:T(8,128)} fusion(bf16[542,768]{1,0:T(8,128)(2,1)S(1)} %copy-done.9, bf16[542,768]{0,1:T(8,128)(2,1)S(1)} %bitcast.76, bf16[542,768]{0,1:T(8,128)(2,1)S(1)} %bitcast.74, bf16[542,768]{0,1:T(8,128)(2,1)S(1)} %bitcast.72), kind=kOutput, calls=%fused_computation.74 | convolution fusion | flops 1925600256 | bytes 10407936 | tf_op jit(solution)/shard_map/dot_general | solution.py:207
  289.3 6.7 %fusion.29 = (f32[768]{0:T(1024)}, f32[542]{0:T(1024)}, f32[542]{0:T(1024)}, f32[542,768]{1,0:T(8,128)}) fusion(bf16[542,768]{1,0:T(8,128)(2,1)} %param.11, f32[768]{0:T(1024)} %param.15, f32[542]{0:T(1024)S(1)} %get-tuple-element.76, f32[542]{0:T(1024)S(1)} %copy-done.27, f32[542]{0:T(1024)S(1)} %broadcast_multiply_fusion.5, f32[768]{0:T(1024)S(1)} %copy-done.33, ...), kind=kOutput, calls=%fused_computation.48 | convolution fusion | flops 1930177280 | bytes 8554072 | tf_op jit(solution)/shard_map/dot_general | solution.py:211
  296.0 40.2 %all-reduce.4 = (f32[768]{0:T(1024)}, f32[768]{0:T(1024)}, f32[768]{0:T(1024)}, f32[3]{0:T(128)}) all-reduce(f32[768]{0:T(1024)} %get-tuple-element.44, f32[768]{0:T(1024)} %convolution_reduce_fusion, f32[768]{0:T(1024)} %get-tuple-element.42, f32[3]{0:T(128)} %pad_maximum_fusion.3), channel_id=1, replica_groups=mesh['dp'=8,'tensor'=4] {'dp','tensor'}, use_global_device_ids=true, to_apply=%region_17.18 | all-reduce | flops 2307 | bytes 18456 | tf_op jit(solution)/shard_map/psum | solution.py:223
  338.7 4.1 fusion.28
  347.4 120.3 %reduce-scatter.7.cloned.1.call-done = f32[24,2304]{1,0:T(8,128)} async-done(((f32[768,2304]{1,0:T(8,128)}), f32[24,2304]{1,0:T(8,128)}) %reduce-scatter.7.cloned.1.call-update) | async-done | bytes 221200 | tf_op jit(solution)/shard_map/reduce_scatter | solution.py:220
  (136 shorter events, 67.9 us)
Async XLA Ops:
  7.2 53.7 %all-gather.7.cloned.1.call-start = ((), (), s32[]{:S(2)}) async-start(), calls=%async_computation.5 | async-start | bytes 4177920 | tf_op jit(solution)/shard_map/all_gather | solution.py:166
  7.9 85.3 %all-gather.5.cloned.1.call-start = ((), (), s32[]{:S(2)}) async-start(), calls=%async_computation.4 | async-start | bytes 4177920 | tf_op jit(solution)/shard_map/all_gather | solution.py:152
  16.9 6.1 %copy-start.32 = (s32[542]{0:T(1024)S(1)}, s32[542]{0:T(1024)}, u32[]{:S(2)}) copy-start(s32[542]{0:T(1024)} %param.13) | copy-start | bytes 6508
  16.9 8.9 %copy-start.34 = (f32[768]{0:T(1024)S(1)}, f32[768]{0:T(1024)}, u32[]{:S(2)}) copy-start(f32[768]{0:T(1024)} %param.15) | copy-start | bytes 9220
  27.8 28.4 %copy-start.25 = (f32[542]{0:T(1024)}, f32[542]{0:T(1024)S(1)}, u32[]{:S(2)}) copy-start(f32[542]{0:T(1024)S(1)} %convert_multiply_fusion.3) | copy-start | bytes 6508
  38.8 8.3 %copy-start.22 = (f32[12,542]{1,0:T(8,128)}, f32[12,542]{1,0:T(8,128)S(1)}, u32[]{:S(2)}) copy-start(f32[12,542]{1,0:T(8,128)S(1)} %get-tuple-element.78) | copy-start | bytes 78052
  38.8 8.3 %copy-start.12 = (bf16[542,768]{0,1:T(8,128)(2,1)S(1)}, bf16[542,768]{0,1:T(8,128)(2,1)}, u32[]{:S(2)}) copy-start(bf16[542,768]{0,1:T(8,128)(2,1)} %copy.49) | copy-start | bytes 2497540
  47.1 9.1 %copy-start.23 = (f32[12,542]{1,0:T(8,128)}, f32[12,542]{1,0:T(8,128)S(1)}, u32[]{:S(2)}) copy-start(f32[12,542]{1,0:T(8,128)S(1)} %fusion.2) | copy-start | bytes 78052
  47.1 9.1 %copy-start.3 = (bf16[542,768]{1,0:T(8,128)(2,1)S(1)}, bf16[542,768]{1,0:T(8,128)(2,1)}, u32[]{:S(2)}) copy-start(bf16[542,768]{1,0:T(8,128)(2,1)} %param.11) | copy-start | bytes 2497540
  47.1 9.0 %copy-start.17 = (bf16[768,768]{1,0:T(8,128)(2,1)S(1)}, bf16[768,768]{1,0:T(8,128)(2,1)}, u32[]{:S(2)}) copy-start(bf16[768,768]{1,0:T(8,128)(2,1)} %param.17) | copy-start | bytes 3538948
  60.7 282.2 %all-reduce.9.cloned.1.call-start = ((), (), s32[]{:S(2)}) async-start(), calls=%async_computation.6 | async-start | bytes 4718592 | tf_op jit(solution)/shard_map/psum | solution.py:182
  97.7 9.2 %copy-start.14 = (bf16[2168,768]{1,0:T(8,128)(2,1)S(1)}, bf16[2168,768]{1,0:T(8,128)(2,1)}, u32[]{:S(2)}) copy-start(bf16[2168,768]{1,0:T(8,128)(2,1)} %reshape.243) | copy-start | bytes 9990148
  106.9 8.8 %copy-start.37 = (f32[2168,768]{1,0:T(8,128)}, f32[2168,768]{1,0:T(8,128)S(1)}, u32[]{:S(2)}) copy-start(f32[2168,768]{1,0:T(8,128)S(1)} %get-tuple-element.82) | copy-start | bytes 19980292
  129.3 218.0 %reduce-scatter.9.cloned.1.call-start = ((), (), s32[]{:S(2)}) async-start(), calls=%async_computation.3 | async-start | bytes 2433024 | tf_op jit(solution)/shard_map/reduce_scatter | solution.py:221
  191.8 10.8 %collective-permute-start = (bf16[6,768]{1,0:T(8,128)(2,1)}, bf16[6,768]{1,0:T(8,128)(2,1)}, u32[]{:S(2)}, u32[]{:S(2)}) collective-permute-start(bf16[6,768]{1,0:T(8,128)(2,1)} %slice.24), channel_id=1, source_target_pairs={{0,1},{1,2},{2,3},{4,5},{5,6},{6,7},{8,9},{9,10},{10,11},{12,13},{... | collective-permute-start | bytes 27656
  195.0 14.5 %collective-permute-start.1 = (bf16[6,768]{1,0:T(8,128)(2,1)}, bf16[6,768]{1,0:T(8,128)(2,1)}, u32[]{:S(2)}, u32[]{:S(2)}) collective-permute-start(bf16[6,768]{1,0:T(8,128)(2,1)} %slice.25), channel_id=1, source_target_pairs={{0,1},{1,2},{2,3},{4,5},{5,6},{6,7},{8,9},{9,10},{10,11},{12,13},{... | collective-permute-start | bytes 27656
  219.7 6.4 %copy-start.18 = (bf16[768,768]{1,0:T(8,128)(2,1)S(1)}, bf16[768,768]{1,0:T(8,128)(2,1)}, u32[]{:S(2)}) copy-start(bf16[768,768]{1,0:T(8,128)(2,1)} %param.17) | copy-start | bytes 3538948
  219.8 6.3 %copy-start.28 = (f32[542]{0:T(1024)S(1)}, f32[542]{0:T(1024)}, u32[]{:S(2)}) copy-start(f32[542]{0:T(1024)} %convert_element_type.93) | copy-start | bytes 6508
  234.6 233.0 %reduce-scatter.7.cloned.1.call-start = ((), (), s32[]{:S(2)}) async-start(), calls=%async_computation.2 | async-start | bytes 7299072 | tf_op jit(solution)/shard_map/reduce_scatter | solution.py:220
  234.6 15.4 %copy-start.21 = (f32[12,542]{1,0:T(8,128)S(1)}, f32[12,542]{1,0:T(8,128)}, u32[]{:S(2)}) copy-start(f32[12,542]{1,0:T(8,128)} %log_add_fusion) | copy-start | bytes 78052
  250.1 12.4 %copy-start.5 = (bf16[542,768]{0,1:T(8,128)(2,1)S(1)}, bf16[542,768]{0,1:T(8,128)(2,1)}, u32[]{:S(2)}) copy-start(bf16[542,768]{0,1:T(8,128)(2,1)} %copy.51) | copy-start | bytes 2497540
  264.2 11.9 %copy-start.15 = (bf16[12,64,542]{2,1,0:T(8,128)(2,1)}, bf16[12,64,542]{2,1,0:T(8,128)(2,1)S(1)}, u32[]{:S(2)}) copy-start(bf16[12,64,542]{2,1,0:T(8,128)(2,1)S(1)} %multiply_convert_fusion.3) | copy-start | bytes 2497540
  266.9 9.1 %copy-start.19 = (bf16[12,64,542]{2,1,0:T(8,128)(2,1)}, bf16[12,64,542]{2,1,0:T(8,128)(2,1)S(1)}, u32[]{:S(2)}) copy-start(bf16[12,64,542]{2,1,0:T(8,128)(2,1)S(1)} %multiply_convert_fusion.2) | copy-start | bytes 2497540
  266.9 10.1 %copy-start.9 = (bf16[542,768]{1,0:T(8,128)(2,1)S(1)}, bf16[542,768]{1,0:T(8,128)(2,1)}, u32[]{:S(2)}) copy-start(bf16[542,768]{1,0:T(8,128)(2,1)} %copy-done.8) | copy-start | bytes 2497540
  (21 other events, 66.6 us)
Sparse Core Ops, SparseCore 0:
  9.6 32.3 all-gather.6
  60.8 32.3 all-gather.4
  129.5 109.0 all-reduce.8
  245.1 98.0 reduce-scatter.8
  349.3 118.2 reduce-scatter.6
where the time goes:
time: 478 us; the launch traced here: 474 us
  waiting for transfers between devices  141 us (29%)
  matrix products  116 us (24%)
  blocking collectives  101 us (21%)
  other arithmetic  54.9 us (11%)
  local copies, waits for them, and re-layouts  40.8 us (9%)
  between operations  15.2 us (3%)
  starting transfers between devices  5.31 us (1%)
    reduce_scatter x1, waiting for transfers between devices, shards(): lax.psum_scatter(grad_qkv, ('dp', 'tensor'), scatter_dimension=0, tiled=T...  120 us
    unnamed x1, blocking collectives  61.1 us
    psum x1, blocking collectives, shards(): lax.psum((grad_gain_one, grad_router, grad_gain_two), ('dp', 'tensor'))  40.2 us
    unnamed x84, local copies, waits for them, and re-layouts  30.1 us
    all_gather x1, waiting for transfers between devices, shards(): gathered = lax.all_gather(low_two, 'tensor', axis=0, tiled=True)  19.7 us
    dot_general x1, matrix products, attend_back(): jnp.einsum('qhd,khd->hqk', grad_heads, values, preferred_element_type=jnp...  15.4 us
    convert_element_type x1, other arithmetic, attend_back(): grad_scores = (attn_prob * (grad_prob - jnp.sum(attn_prob * grad_prob, ax...  12.3 us
    dot_general x1, matrix products, masked_scores(): jnp.einsum('qhd,khd->hqk', queries, key_heads, preferred_element_type=jnp...  10 us
  transfers between devices with their start and end apart: 7, of which 2 were waited for; matrix products, arithmetic and copies ran while one was open for 49% of the time, Pallas kernels for 0%

commit v1 on v0

v1 whole, which is shorter than its diff:
```python
import math

import jax
import jax.numpy as jnp
from jax import lax
from jax.experimental import pallas as pl
from jax.experimental.pallas import tpu as pltpu
from jax.sharding import PartitionSpec as P

HEADS = 12
HEAD_DIM = 64
PAIR = 2 * HEAD_DIM
EPSILON = 1e-06
NEGATIVE = -1000000000.0
GELU_C = math.sqrt(2.0 / math.pi)
GELU_A = 0.044715
F32 = jnp.float32
BF16 = jnp.bfloat16
VMEM_LIMIT = 60 * 1024 * 1024
ALL = ("dp", "tensor")


def dot_nn(a, b):
    return lax.dot_general(a, b, (((1,), (0,)), ((), ())), preferred_element_type=F32)


def dot_nt(a, b):
    return lax.dot_general(a, b, (((1,), (1,)), ((), ())), preferred_element_type=F32)


def dot_tn(a, b):
    return lax.dot_general(a, b, (((0,), (0,)), ((), ())), preferred_element_type=F32)


def iota(shape, dim):
    return lax.broadcasted_iota(jnp.int32, shape, dim)


def norm_rows(rows, gain):
    center = rows - jnp.mean(rows, axis=-1, keepdims=True)
    inverse = lax.rsqrt(jnp.mean(center * center, axis=-1, keepdims=True) + EPSILON)
    unit = center * inverse
    return unit * gain, unit, inverse


def norm_back(grad_out, unit, inverse, gain):
    scaled = grad_out * gain
    mean_grad = jnp.mean(scaled, axis=-1, keepdims=True)
    mean_cross = jnp.mean(scaled * unit, axis=-1, keepdims=True)
    grad_in = inverse * (scaled - mean_grad - unit * mean_cross)
    return grad_in, jnp.sum(grad_out * unit, axis=0, keepdims=True)


def call(body, outs, name, flops=0, moved=0, scratch=(), n_in=None, smem=()):
    vmem = pl.BlockSpec(memory_space=pltpu.VMEM)
    scalar = pl.BlockSpec(memory_space=pltpu.SMEM)
    return pl.pallas_call(
        body,
        out_shape=tuple(jax.ShapeDtypeStruct(s, d) for s, d in outs),
        in_specs=[scalar if i in smem else vmem for i in range(n_in)],
        out_specs=tuple(vmem for _ in outs),
        scratch_shapes=list(scratch),
        compiler_params=pltpu.CompilerParams(vmem_limit_bytes=VMEM_LIMIT),
        cost_estimate=pl.CostEstimate(flops=flops, bytes_accessed=moved, transcendentals=0),
        name=name,
    )


def places(cap, rows, half, blk):
    k, j = iota((rows, rows), 0), iota((rows, rows), 1)
    cap_col = jnp.sum(jnp.where(k == j, cap, 0.0), axis=1, keepdims=True)
    rank_row = jnp.sum(jnp.where(k < j, cap_col, 0.0), axis=0, keepdims=True)
    rank_col = jnp.sum(jnp.where(j < k, cap, 0.0), axis=1, keepdims=True)
    at_row = iota((1, rows), 1).astype(F32)
    at_col = iota((rows, 1), 0).astype(F32)
    dest_row = jnp.where(cap > 0.5, rank_row, blk + at_row - rank_row)
    dest_col = jnp.where(cap_col > 0.5, rank_col, blk + at_col - rank_col)
    return dest_row.astype(jnp.int32), dest_col.astype(jnp.int32)


def pre_body(tok, cot, cap, lens, gain2, xc, xn, cc, cn, n2n, bias):
    rows = tok.shape[0]
    blk = xc.shape[0]
    dest_row, _ = places(cap[...].astype(F32), rows, rows // 2, blk)
    pick = (iota((2 * blk, rows), 0) == dest_row).astype(BF16)
    x = dot_nn(pick, tok[...])
    c = dot_nn(pick, cot[...])
    xc[...] = x[:blk].astype(BF16)
    xn[...] = x[blk:].astype(BF16)
    cc[...] = c[:blk].astype(BF16)
    cn[...] = c[blk:].astype(BF16)
    n2n[...] = norm_rows(x[blk:], gain2[...])[0].astype(BF16)
    position = iota((1, rows), 1)
    crop = jnp.ones((1, rows), F32)
    end = 0
    for s in range(lens.shape[1]):
        end = end + lens[0, s]
        crop = crop + (position >= end).astype(F32)
    crop_col = jnp.sum(jnp.where(iota((blk, rows), 0) == dest_row, crop, 0.0), axis=1, keepdims=True)
    crop_row = jnp.sum(
        jnp.where(iota((blk, blk), 0) == iota((blk, blk), 1), crop_col, 0.0), axis=0, keepdims=True
    )
    bias[...] = jnp.where(crop_col == crop_row, 0.0, NEGATIVE)


def half_mask(shape, e):
    return (iota(shape, 1) < HEAD_DIM) == (e == 0)


def fore_body(
    half,
    xc, bias, gain1, router, w_qkv, w_out, gain2,
    n1, qkv, probs, heads, attended, gate, n2c, stats,
):
    blk, width = xc.shape
    x = xc[...].astype(F32)
    low = norm_rows(x, gain1[...])[0].astype(BF16)
    n1[...] = low
    logit = jnp.sum(low.astype(F32) * router[...], axis=-1, keepdims=True)
    gated = jnp.where(iota((blk, 1), 0) < half, jax.nn.sigmoid(logit), 0.0)
    gate[...] = gated
    qkv[...] = dot_nn(low, w_qkv[...]).astype(BF16)
    scale = 1.0 / math.sqrt(HEAD_DIM)
    for pair in range(HEADS // 2):
        at = pair * PAIR
        q = qkv[:, at : at + PAIR]
        k = qkv[:, width + at : width + at + PAIR]
        v = qkv[:, 2 * width + at : 2 * width + at + PAIR]
        total = None
        for e in range(2):
            mask = half_mask((blk, PAIR), e)
            zero = jnp.zeros_like(q)
            scores = dot_nt(jnp.where(mask, q, zero), k) * scale + bias[...]
            exponent = jnp.exp(scores - jnp.max(scores, axis=-1, keepdims=True))
            prob = (exponent / jnp.sum(exponent, axis=-1, keepdims=True)).astype(BF16)
            probs[2 * pair + e] = prob
            part = dot_nn(prob, jnp.where(mask, v, zero))
            total = part if total is None else total + part
        heads[:, at : at + PAIR] = total.astype(BF16)
    att = dot_nn(heads[...], w_out[...])
    attended[...] = att
    branch = gated * att
    resid = x + branch
    n2c[...] = norm_rows(resid, gain2[...])[0].astype(BF16)
    stats[0:1, :] = jnp.sum(resid * resid, axis=0, keepdims=True)
    stats[1:2, :] = jnp.sum(branch * branch, axis=0, keepdims=True)


def mlp_body(sources, blk, *refs):
    n2s, cots = refs[:sources], refs[sources : 2 * sources]
    w_up, w_down = refs[2 * sources : 2 * sources + 2]
    outs = refs[2 * sources + 2 :]
    hidden, d_n2, g_up, g_down, n2, cot, act, dpre = outs
    for s in range(sources):
        n2[s * blk : (s + 1) * blk] = n2s[s][...]
        cot[s * blk : (s + 1) * blk] = cots[s][...]

    @pl.loop(0, sources)
    def _(s):
        rows = pl.ds(pl.multiple_of(s * blk, 16), blk)
        pre = dot_nn(n2[rows, :], w_up[...])
        d_act = dot_nt(cot[rows, :], w_down[...])
        square = pre * pre
        t = jnp.tanh(GELU_C * pre * (1.0 + GELU_A * square))
        half_up = 0.5 * (1.0 + t)
        slope = half_up + 0.5 * pre * (1.0 - t * t) * (GELU_C * (1.0 + 3.0 * GELU_A * square))
        a = (pre * half_up).astype(BF16)
        d = (d_act * slope).astype(BF16)
        act[rows, :] = a
        dpre[rows, :] = d
        hidden[rows, :] = dot_nn(a, w_down[...]).astype(BF16)
        d_n2[rows, :] = dot_nt(d, w_up[...]).astype(BF16)

    tile = 256

    @pl.loop(0, g_up.shape[1] // tile)
    def _(n):
        cols = pl.ds(pl.multiple_of(n * tile, tile), tile)
        g_up[:, cols] = dot_tn(n2[...], dpre[:, cols]).astype(BF16)
        g_down[cols, :] = dot_tn(act[:, cols], cot[...]).astype(BF16)


def back_body(
    half,
    d_n2, cc, xc, attended, gate, heads, qkv, probs, n1, w_qkv, w_out, gain1, gain2, router,
    grad_in, g_qkv, g_proj, gains, d_qkv,
):
    blk, width = xc.shape
    scale = 1.0 / math.sqrt(HEAD_DIM)
    x = xc[...].astype(F32)
    gated = gate[...]
    resid = x + gated * attended[...]
    _, unit2, inverse2 = norm_rows(resid, gain2[...])
    back2, g_gain2 = norm_back(d_n2[...].astype(F32), unit2, inverse2, gain2[...])
    d_resid = cc[...].astype(F32) + back2
    d_att = (d_resid * gated).astype(BF16)
    keep = (iota((blk, 1), 0) < half).astype(F32)
    d_gate = keep * jnp.sum(d_resid * attended[...], axis=-1, keepdims=True)
    d_logit = d_gate * gated * (1.0 - gated)
    g_proj[...] = dot_tn(heads[...], d_att).astype(BF16)
    d_heads = dot_nt(d_att, w_out[...]).astype(BF16)
    for pair in range(HEADS // 2):
        at = pair * PAIR
        q = qkv[:, at : at + PAIR]
        k = qkv[:, width + at : width + at + PAIR]
        v = qkv[:, 2 * width + at : 2 * width + at + PAIR]
        d_o = d_heads[:, at : at + PAIR]
        zero = jnp.zeros_like(q)
        d_q = d_k = d_v = 0.0
        for e in range(2):
            mask = half_mask((blk, PAIR), e)
            d_oe = jnp.where(mask, d_o, zero)
            prob = probs[2 * pair + e]
            prob_f = prob.astype(F32)
            d_prob = dot_nt(d_oe, v)
            d_score = (
                prob_f * (d_prob - jnp.sum(prob_f * d_prob, axis=-1, keepdims=True))
            ).astype(BF16)
            d_v = d_v + dot_tn(prob, d_oe)
            d_q = d_q + dot_nn(d_score, jnp.where(mask, k, zero))
            d_k = d_k + dot_tn(d_score, jnp.where(mask, q, zero))
        d_qkv[:, at : at + PAIR] = (d_q * scale).astype(BF16)
        d_qkv[:, width + at : width + at + PAIR] = (d_k * scale).astype(BF16)
        d_qkv[:, 2 * width + at : 2 * width + at + PAIR] = d_v.astype(BF16)
    low = n1[...]
    g_qkv[...] = dot_tn(low, d_qkv[...]).astype(BF16)
    d_n1 = dot_nt(d_qkv[...], w_qkv[...]) + d_logit * router[...]
    _, unit1, inverse1 = norm_rows(x, gain1[...])
    back1, g_gain1 = norm_back(d_n1, unit1, inverse1, gain1[...])
    grad_in[...] = d_resid + back1
    gains[0:1, :] = g_gain1
    gains[1:2, :] = jnp.sum(d_logit * low.astype(F32), axis=0, keepdims=True)
    gains[2:3, :] = g_gain2


def put_back(pick, rows):
    top = rows.astype(BF16)
    rest = (rows - top.astype(F32)).astype(BF16)
    return dot_nn(pick, top) + dot_nn(pick, rest)


def post_body(
    cap, hidden_c, hidden_n, d_n2n, xc, xn, cn, attended, gate, grad_in_c, gain2,
    mixed, grad_in, stats,
):
    rows = mixed.shape[0]
    blk = xc.shape[0]
    _, dest_col = places(cap[...].astype(F32), rows, rows // 2, blk)
    pick_c = (iota((rows, blk), 1) == dest_col).astype(BF16)
    pick_n = (iota((rows, blk), 1) + blk == dest_col).astype(BF16)
    h_c, h_n = hidden_c[...].astype(F32), hidden_n[...].astype(F32)
    x_n = xn[...].astype(F32)
    mix_c = (xc[...].astype(F32) + gate[...] * attended[...] + h_c).astype(BF16)
    mix_n = (x_n + h_n).astype(BF16)
    mixed[...] = (dot_nn(pick_c, mix_c) + dot_nn(pick_n, mix_n)).astype(BF16)
    _, unit, inverse = norm_rows(x_n, gain2[...])
    back, g_gain2 = norm_back(d_n2n[...].astype(F32), unit, inverse, gain2[...])
    d_resid = cn[...].astype(F32) + back
    grad_in[...] = put_back(pick_c, grad_in_c[...]) + put_back(pick_n, d_resid)
    stats[0:1, :] = g_gain2
    stats[1:2, :] = jnp.sum(x_n * x_n, axis=0, keepdims=True)
    stats[2:3, :] = jnp.sum(h_c * h_c, axis=0, keepdims=True) + jnp.sum(
        h_n * h_n, axis=0, keepdims=True
    )


CORES = 2


def tensor_shift(array, size, dy, dc):
    steps = [
        (y * CORES + c, ((y + dy) % (size // CORES)) * CORES + (c ^ dc))
        for y in range(size // CORES)
        for c in range(CORES)
    ]
    return lax.ppermute(array, "tensor", steps)


def gather_rows(array, size):
    held = [array] + [tensor_shift(array, size, dy, 0) for dy in range(1, size // CORES)]
    out = []
    for a in held:
        out += [a, tensor_shift(a, size, 0, 1)]
    return out


def scatter_rows(parts, size):
    total = None
    for dy in range(size // CORES):
        other = tensor_shift(parts[2 * dy + 1], size, 0, 1)
        joint = parts[2 * dy].astype(F32) + other.astype(F32)
        if dy:
            joint = tensor_shift(joint.astype(BF16), size, -dy, 0).astype(F32)
        total = joint if total is None else total + joint
    return total


def shards(
    tokens, lengths, capacity, norm1_gain, router, w_qkv, w_out, norm2_gain, w_up, w_down, cotangent
):
    rows, width = tokens.shape
    half = rows // 2
    blk = -(-half // 16) * 16
    hidden_units = w_up.shape[1]
    tsize = lax.axis_size("tensor")
    cap = capacity.reshape(1, rows)
    gain1, gain2, route = (a.reshape(1, width) for a in (norm1_gain, norm2_gain, router))
    small = (blk, width)

    xc, xn, cc, cn, n2n, bias = call(
        pre_body,
        [(small, BF16)] * 5 + [((blk, blk), F32)],
        "pre",
        flops=4 * 2 * blk * rows * width,
        moved=8 * rows * width,
        n_in=5,
        smem=(3,),
    )(tokens, cotangent, cap, lengths, gain2)

    cc_all = gather_rows(cc, tsize)
    cn_all = gather_rows(cn, tsize)
    n2n_all = gather_rows(n2n, tsize)

    n1, qkv, probs, heads, attended, gate, n2c, stats1 = call(
        lambda *refs: fore_body(half, *refs),
        [
            (small, BF16), ((blk, 3 * width), BF16), ((HEADS, blk, blk), BF16), (small, BF16),
            (small, F32), ((blk, 1), F32), (small, BF16), ((2, width), F32),
        ],
        "fore",
        flops=2 * blk * width * 4 * width + 4 * blk * blk * width * 4,
        moved=4 * width * width * 2 + 20 * blk * width,
        n_in=7,
    )(xc, bias, gain1, route, w_qkv, w_out, gain2)

    n2c_all = gather_rows(n2c, tsize)

    sources = 2 * tsize
    tall = (sources * blk, width)
    hidden_p, d_n2_p, g_up, g_down = call(
        lambda *refs: mlp_body(sources, blk, *refs),
        [(tall, BF16), (tall, BF16), ((width, hidden_units), BF16), ((hidden_units, width), BF16)],
        "mlp",
        flops=12 * sources * blk * width * hidden_units,
        moved=8 * sources * blk * width,
        scratch=[
            pltpu.VMEM(tall, BF16), pltpu.VMEM(tall, BF16),
            pltpu.VMEM((sources * blk, hidden_units), BF16), pltpu.VMEM((sources * blk, hidden_units), BF16),
        ],
        n_in=2 * sources + 2,
    )(*n2c_all, *n2n_all, *cc_all, *cn_all, w_up, w_down)

    def cut(array, s):
        return array[s * blk : (s + 1) * blk]

    d_n2c = scatter_rows([cut(d_n2_p, s) for s in range(tsize)], tsize)
    d_n2n = scatter_rows([cut(d_n2_p, tsize + s) for s in range(tsize)], tsize)
    hidden_c = scatter_rows([cut(hidden_p, s) for s in range(tsize)], tsize)
    hidden_n = scatter_rows([cut(hidden_p, tsize + s) for s in range(tsize)], tsize)

    g_up, g_down = lax.psum((g_up, g_down), "dp")

    grad_in_c, g_qkv, g_proj, gains = call(
        lambda *refs: back_body(half, *refs),
        [(small, F32), ((width, 3 * width), BF16), ((width, width), BF16), ((3, width), F32)],
        "back",
        flops=4 * blk * width * 4 * width + 8 * blk * blk * width * 4,
        moved=8 * width * width * 2 + 20 * blk * width,
        scratch=[pltpu.VMEM((blk, 3 * width), BF16)],
        n_in=14,
    )(d_n2c, cc, xc, attended, gate, heads, qkv, probs, n1, w_qkv, w_out, gain1, gain2, route)

    qkv_share, proj_share = (
        lax.psum_scatter(g, ALL, scatter_dimension=0, tiled=True).astype(F32)
        for g in (g_qkv, g_proj)
    )

    mixed, grad_input, stats2 = call(
        post_body,
        [((rows, width), BF16), ((rows, width), F32), ((3, width), F32)],
        "post",
        flops=6 * 2 * rows * blk * width,
        moved=20 * rows * width,
        n_in=11,
    )(cap, hidden_c, hidden_n, d_n2n, xc, xn, cn, attended, gate, grad_in_c, gain2)

    sums = jnp.stack(
        [
            gains[0],
            gains[1],
            gains[2] + stats2[0],
            stats1[0] + stats2[1],
            stats1[1],
            stats2[2],
        ]
    )
    sums = lax.psum(sums, ALL)
    count = rows * width * lax.axis_size("dp") * lax.axis_size("tensor")
    norms = jnp.sqrt(jnp.sum(sums[3:], axis=-1) / count)
    return (
        mixed,
        grad_input,
        sums[0],
        sums[1],
        qkv_share,
        proj_share,
        sums[2],
        g_up.astype(F32),
        g_down.astype(F32),
        norms,
    )


def solution(mesh):
    return jax.shard_map(
        shards,
        mesh=mesh,
        in_specs=(
            P(("dp", "tensor"), None),
            P(("dp", "tensor"), None),
            P(("dp", "tensor")),
            P(),
            P(),
            P(),
            P(),
            P(),
            P(None, "tensor"),
            P("tensor", None),
            P(("dp", "tensor"), None),
        ),
        out_specs=(
            P(("dp", "tensor"), None),
            P(("dp", "tensor"), None),
            P(),
            P(),
            P(("dp", "tensor"), None),
            P(("dp", "tensor"), None),
            P(),
            P(None, "tensor"),
            P("tensor", None),
            P(),
        ),
        check_vma=False,
    )
```

time: 478 us -> 358 us (0.75)
  matrix products: 116 us -> 0 us
  Pallas kernels: 0 us -> 59.8 us
  blocking collectives: 101 us -> 43 us
  waiting for transfers between devices: 141 us -> 199 us
  other arithmetic: 54.9 us -> 13.8 us
  local copies, waits for them, and re-layouts: 40.8 us -> 10.9 us
  starting transfers between devices: 5.31 us -> 15.4 us
    dot_general x20 -> x0, matrix products: 116 us -> none  [the longest x1 15.4 us: attend_back(): jnp.einsum('qhd,khd->hqk', grad_heads, values, preferred_element_type=jnp...]
    ppermute x0 -> x24, waiting for transfers between devices: none -> 72.3 us  [tensor_shift(): return lax.ppermute(array, 'tensor', steps)]
    unnamed x1 -> x0, blocking collectives: 61.1 us -> none
    pallas_call x0 -> x5, Pallas kernels: none -> 59.8 us  [the longest x1 24.2 us: shards(): call(lambda *refs: mlp_body(sources, blk, *refs), [(tall, BF16), (tall, B...]
    unnamed x84 -> x42, local copies, waits for them, and re-layouts: 30.1 us -> 1.07 us
    reduce_sum x7 -> x1, other arithmetic: 21.1 us -> 0.12 us  [shards(): norms = jnp.sqrt(jnp.sum(sums[3:], axis=-1) / count)]
    all_gather x2 -> x0, waiting for transfers between devices: 19.8 us -> none  [the longest x1 19.7 us: shards(): gathered = lax.all_gather(low_two, 'tensor', axis=0, tiled=True)]
    ppermute x0 -> x24, starting transfers between devices: none -> 14.9 us  [tensor_shift(): return lax.ppermute(array, 'tensor', steps)]
  transfers between devices with their start and end apart: 7 -> 27, of which waited for: 2 -> 13; matrix products, arithmetic and copies ran while one was open for 49% -> 5% of each run, Pallas kernels for 0% -> 6%
where the time goes in v1:
time: 358 us; the launch traced here: 357 us
  waiting for transfers between devices  199 us (56%)
  Pallas kernels  59.8 us (17%)
  blocking collectives  43 us (12%)
  between operations  15.7 us (4%)
  starting transfers between devices  15.4 us (4%)
  other arithmetic  13.8 us (4%)
  local copies, waits for them, and re-layouts  10.9 us (3%)
    reduce_scatter x2, waiting for transfers between devices, shards(): lax.psum_scatter(g, ALL, scatter_dimension=0, tiled=True).astype(F32)  126 us
    ppermute x24, waiting for transfers between devices, tensor_shift(): return lax.ppermute(array, 'tensor', steps)  72.3 us
    psum x1, blocking collectives, shards(): sums = lax.psum(sums, ALL)  43 us
    pallas_call x1, Pallas kernels, shards(): call(lambda *refs: mlp_body(sources, blk, *refs), [(tall, BF16), (tall, B...  24.2 us
    pallas_call x1, Pallas kernels, shards(): call(lambda *refs: back_body(half, *refs), [(small, F32), ((width, 3 * wi...  15.6 us
    ppermute x24, starting transfers between devices, tensor_shift(): return lax.ppermute(array, 'tensor', steps)  14.9 us
    pallas_call x1, Pallas kernels, shards(): call(lambda *refs: fore_body(half, *refs), [(small, BF16), ((blk, 3 * wid...  8.97 us
  transfers between devices with their start and end apart: 27, of which 13 were waited for; matrix products, arithmetic and copies ran while one was open for 5% of the time, Pallas kernels for 6%

profile of v1, /device:TPU:0, one launch (start us, length us, event | category | flops | bytes accessed | tf_op | source)
XLA Modules:
  0.0 357.4 jit_solution(10930379426764110670)
XLA Ops:
  13.1 4.1 %pre.1 = (bf16[272,768]{1,0:T(8,128)(2,1)}, bf16[272,768]{1,0:T(8,128)(2,1)}, bf16[272,768]{1,0:T(8,128)(2,1)}, bf16[272,768]{1,0:T(8,128)(2,1)}, bf16[272,768]{1,0:T(8,128)(2,1)}, /*index=5*/f32[272,272]{1,0:T(8,128)}) custom-call(bf16[542,768]{1,0:T(8,128)(2,1)} %tok.1, bf16[542,768]{1,0:T(8,128)(2,1)} %cot.1, s32[1,542]{1,0:T(1,128)} %reshape.32.cap, ...), custom_call_target="tpu_custom_call" | custom-call | flops 905773056 | bytes 3330048 | tf_op jit(solution)/shard_map/pre/pallas_call | solution.py:310
  17.3 9.0 %fore.1 = (bf16[272,768]{1,0:T(8,128)(2,1)}, bf16[272,2304]{1,0:T(8,128)(2,1)}, bf16[12,272,272]{2,1,0:T(8,128)(2,1)}, bf16[272,768]{1,0:T(8,128)(2,1)}, f32[272...) custom-call(bf16[272,768]{1,0:T(8,128)(2,1)} %get-tuple-element.35.refs_0_.refs_2_.xc, ...), custom_call_target="tpu_custom_call" | custom-call | flops 2192572416 | bytes 8896512 | tf_op jit(solution)/shard_map/fore/pallas_call | solution.py:324
  26.7 2.6 collective-permute-start.1
  29.8 1.8 collective-permute-start.7
  31.5 8.4 %collective-permute-done.1.refs_2_ = bf16[272,768]{1,0:T(8,128)(2,1)S(1)} collective-permute-done((bf16[272,768]{1,0:T(8,128)(2,1)}, bf16[272,768]{1,0:T(8,128)(2,1)S(1)}, u32[]{:S(2)}, u32[]{:S(2)}) %collective-permute-start.1) | collective-permute-done | bytes 417824 | tf_op jit(solution)/shard_map/ppermute | solution.py:276
  40.0 2.0 collective-permute-start.10
  41.9 7.0 %collective-permute-done.4.refs_6_ = bf16[272,768]{1,0:T(8,128)(2,1)S(1)} collective-permute-done((bf16[272,768]{1,0:T(8,128)(2,1)S(1)}, bf16[272,768]{1,0:T(8,128)(2,1)S(1)}, u32[]{:S(2)}, u32[]{:S(2)}) %collective-permute-start.4) | collective-permute-done | bytes 417824 | tf_op jit(solution)/shard_map/ppermute | solution.py:276
  49.4 8.4 %collective-permute-done.7.refs_10_ = bf16[272,768]{1,0:T(8,128)(2,1)S(1)} collective-permute-done((bf16[272,768]{1,0:T(8,128)(2,1)S(1)}, bf16[272,768]{1,0:T(8,128)(2,1)S(1)}, u32[]{:S(2)}, u32[]{:S(2)}) %collective-permute-start.7) | collective-permute-done | bytes 417824 | tf_op jit(solution)/shard_map/ppermute | solution.py:276
  57.9 8.7 %collective-permute-done.10.refs_14_ = bf16[272,768]{1,0:T(8,128)(2,1)S(1)} collective-permute-done((bf16[272,768]{1,0:T(8,128)(2,1)S(1)}, bf16[272,768]{1,0:T(8,128)(2,1)S(1)}, u32[]{:S(2)}, u32[]{:S(2)}) %collective-permute-start.10) | collective-permute-done | bytes 417824 | tf_op jit(solution)/shard_map/ppermute | solution.py:276
  68.5 24.2 %mlp.1 = (bf16[2176,768]{1,0:T(8,128)(2,1)}, bf16[2176,768]{1,0:T(8,128)(2,1)}, bf16[768,768]{1,0:T(8,128)(2,1)}, bf16[768,768]{1,0:T(8,128)(2,1)}) custom-call(bf16[272,768]{1,0:T(8,128)(2,1)} %get-tuple-element.37.refs_0_, bf16[272,768]{1,0:T(8,128)(2,1)} %copy-done.10, bf16[272,768]{1,0:T(8,128)(2,1)} %copy-done.11, bf16[272,768]{1,0:T(8,128)(2,1)} %copy-done.18, ...), custom_call_target="tpu_custom_call" | custom-call | flops 15401484288 | bytes 13369344 | tf_op jit(solution)/shard_map/mlp/pallas_call | solution.py:340
  92.9 2.4 fusion
  97.2 1.8 collective-permute-start.23
  99.0 10.0 %collective-permute-done.23 = bf16[272,768]{1,0:T(8,128)(2,1)S(1)} collective-permute-done((bf16[272,768]{1,0:T(8,128)(2,1)S(1)}, bf16[272,768]{1,0:T(8,128)(2,1)S(1)}, u32[]{:S(2)}, u32[]{:S(2)}) %collective-permute-start.23) | collective-permute-done | bytes 417824 | tf_op jit(solution)/shard_map/ppermute | solution.py:276
  110.4 15.6 %back.1 = (f32[272,768]{1,0:T(8,128)}, bf16[768,2304]{1,0:T(8,128)(2,1)}, bf16[768,768]{1,0:T(8,128)(2,1)}, f32[3,768]{1,0:T(4,128)}) custom-call(f32[272,768]{1,0:T(8,128)} %get-tuple-element.65.refs_0_, bf16[272,768]{1,0:T(8,128)(2,1)} %get-tuple-element.39.refs_8_.refs_1_, bf16[272,768]{1,0:T(8,128)(2,1)} %get-tuple-element.35.refs_0_.refs_2_.xc, ...), custom_call_target="tpu_custom_call" | custom-call | flops 4385144832 | bytes 13615104 | tf_op jit(solution)/shard_map/back/pallas_call | solution.py:363
  130.3 1.8 collective-permute-start.17
  132.1 9.9 %collective-permute-done.17 = bf16[272,768]{1,0:T(8,128)(2,1)S(1)} collective-permute-done((bf16[272,768]{1,0:T(8,128)(2,1)S(1)}, bf16[272,768]{1,0:T(8,128)(2,1)S(1)}, u32[]{:S(2)}, u32[]{:S(2)}) %collective-permute-start.17) | collective-permute-done | bytes 417824 | tf_op jit(solution)/shard_map/ppermute | solution.py:276
  143.2 1.7 collective-permute-start.14
  145.4 10.5 %collective-permute-done.14 = bf16[272,768]{1,0:T(8,128)(2,1)S(1)} collective-permute-done((bf16[272,768]{1,0:T(8,128)(2,1)S(1)}, bf16[272,768]{1,0:T(8,128)(2,1)S(1)}, u32[]{:S(2)}, u32[]{:S(2)}) %collective-permute-start.14) | collective-permute-done | bytes 417824 | tf_op jit(solution)/shard_map/ppermute | solution.py:276
  156.9 6.3 %collective-permute-done.20 = bf16[272,768]{1,0:T(8,128)(2,1)S(1)} collective-permute-done((bf16[272,768]{1,0:T(8,128)(2,1)S(1)}, bf16[272,768]{1,0:T(8,128)(2,1)S(1)}, u32[]{:S(2)}, u32[]{:S(2)}) %collective-permute-start.20) | collective-permute-done | bytes 417824 | tf_op jit(solution)/shard_map/ppermute | solution.py:276
  164.2 6.9 %post.1 = (bf16[542,768]{1,0:T(8,128)(2,1)}, f32[542,768]{1,0:T(8,128)}, f32[3,768]{1,0:T(4,128)}) custom-call(s32[1,542]{1,0:T(1,128)} %reshape.32.cap, f32[272,768]{1,0:T(8,128)} %convert_add_fusion.3.hidden_c, f32[272,768]{1,0:T(8,128)} %get-tuple-element.71.hidden_n, f32[272,768]{1,0:T(8,128)} %convert_add_fusion.1.d_n2n, ...), custom_call_target="tpu_custom_call" | custom-call | flops 1358659584 | bytes 8325120 | tf_op jit(solution)/shard_map/post/pallas_call | solution.py:378
  172.0 43.0 %psum.21 = f32[6,768]{1,0:T(8,128)S(1)} all-reduce(f32[6,768]{1,0:T(8,128)S(1)} %stack.6), channel_id=1, replica_groups=mesh['dp'=8,'tensor'=4] {'dp','tensor'}, use_global_device_ids=true, to_apply=%region_0.0 | all-reduce | flops 4608 | bytes 36864 | tf_op jit(solution)/shard_map/psum | solution.py:397
  216.2 2.9 convert_element_type.110
  220.8 20.3 %reduce-scatter.5.cloned.1.call-done = bf16[24,768]{1,0:T(8,128)(2,1)} async-done(((bf16[768,768]{1,0:T(8,128)(2,1)}), bf16[24,768]{1,0:T(8,128)(2,1)}) %reduce-scatter.5.cloned.1.call-update) | async-done | bytes 36880 | tf_op jit(solution)/shard_map/reduce_scatter | solution.py:374
  242.5 105.9 %reduce-scatter.3.cloned.1.call-done = bf16[24,2304]{1,0:T(8,128)(2,1)} async-done(((bf16[768,2304]{1,0:T(8,128)(2,1)}), bf16[24,2304]{1,0:T(8,128)(2,1)}) %reduce-scatter.3.cloned.1.call-update) | async-done | bytes 110608 | tf_op jit(solution)/shard_map/reduce_scatter | solution.py:374
  (103 shorter events, 26.5 us)
Async XLA Ops:
  8.0 208.2 %all-reduce.3.cloned.1.call-start = ((), (), s32[]{:S(2)}) async-start(), calls=%async_computation.4 | async-start | bytes 4718592 | tf_op jit(solution)/shard_map/psum | solution.py:361
  26.2 3.6 collective-permute-start
  26.7 13.3 %collective-permute-start.1 = (bf16[272,768]{1,0:T(8,128)(2,1)}, bf16[272,768]{1,0:T(8,128)(2,1)S(1)}, u32[]{:S(2)}, u32[]{:S(2)}) collective-permute-start(bf16[272,768]{1,0:T(8,128)(2,1)} %get-tuple-element.37.refs_0_), channel_id=1, source_target_pairs={{0,2},{1,3},{2,0},{3,1},{4,6},{5,7},{6,4},{7,5},{8,10},{9,11},{10,... | collective-permute-start | bytes 1253384 | tf_op jit(solution)/shard_map/ppermute | solution.py:276
  29.3 12.7 %collective-permute-start.3 = (bf16[272,768]{1,0:T(8,128)(2,1)S(1)}, bf16[272,768]{1,0:T(8,128)(2,1)S(1)}, u32[]{:S(2)}, u32[]{:S(2)}) collective-permute-start(bf16[272,768]{1,0:T(8,128)(2,1)S(1)} %copy-done.9), channel_id=1, source_target_pairs={{0,1},{1,0},{2,3},{3,2},{4,5},{5,4},{6,7},{7,6},{8,9},{9,8},{10,11... | collective-permute-start | bytes 1253384 | tf_op jit(solution)/shard_map/ppermute | solution.py:276
  29.4 19.5 %collective-permute-start.4 = (bf16[272,768]{1,0:T(8,128)(2,1)S(1)}, bf16[272,768]{1,0:T(8,128)(2,1)S(1)}, u32[]{:S(2)}, u32[]{:S(2)}) collective-permute-start(bf16[272,768]{1,0:T(8,128)(2,1)S(1)} %copy-done.9), channel_id=1, source_target_pairs={{0,2},{1,3},{2,0},{3,1},{4,6},{5,7},{6,4},{7,5},{8,10},{9,11},{10,... | collective-permute-start | bytes 1253384 | tf_op jit(solution)/shard_map/ppermute | solution.py:276
  29.7 19.2 %collective-permute-start.6 = (bf16[272,768]{1,0:T(8,128)(2,1)S(1)}, bf16[272,768]{1,0:T(8,128)(2,1)S(1)}, u32[]{:S(2)}, u32[]{:S(2)}) collective-permute-start(bf16[272,768]{1,0:T(8,128)(2,1)S(1)} %copy-done.8), channel_id=1, source_target_pairs={{0,1},{1,0},{2,3},{3,2},{4,5},{5,4},{6,7},{7,6},{8,9},{9,8},{10,11... | collective-permute-start | bytes 1253384 | tf_op jit(solution)/shard_map/ppermute | solution.py:276
  29.8 28.1 %collective-permute-start.7 = (bf16[272,768]{1,0:T(8,128)(2,1)S(1)}, bf16[272,768]{1,0:T(8,128)(2,1)S(1)}, u32[]{:S(2)}, u32[]{:S(2)}) collective-permute-start(bf16[272,768]{1,0:T(8,128)(2,1)S(1)} %copy-done.8), channel_id=1, source_target_pairs={{0,2},{1,3},{2,0},{3,1},{4,6},{5,7},{6,4},{7,5},{8,10},{9,11},{10,... | collective-permute-start | bytes 1253384 | tf_op jit(solution)/shard_map/ppermute | solution.py:276
  40.0 26.6 %collective-permute-start.10 = (bf16[272,768]{1,0:T(8,128)(2,1)S(1)}, bf16[272,768]{1,0:T(8,128)(2,1)S(1)}, u32[]{:S(2)}, u32[]{:S(2)}) collective-permute-start(bf16[272,768]{1,0:T(8,128)(2,1)S(1)} %copy-done.5), channel_id=1, source_target_pairs={{0,2},{1,3},{2,0},{3,1},{4,6},{5,7},{6,4},{7,5},{8,10},{9,11},{10,... | collective-permute-start | bytes 1253384 | tf_op jit(solution)/shard_map/ppermute | solution.py:276
  41.9 24.7 %collective-permute-start.9 = (bf16[272,768]{1,0:T(8,128)(2,1)S(1)}, bf16[272,768]{1,0:T(8,128)(2,1)S(1)}, u32[]{:S(2)}, u32[]{:S(2)}) collective-permute-start(bf16[272,768]{1,0:T(8,128)(2,1)S(1)} %copy-done.5), channel_id=1, source_target_pairs={{0,1},{1,0},{2,3},{3,2},{4,5},{5,4},{6,7},{7,6},{8,9},{9,8},{10,11... | collective-permute-start | bytes 1253384 | tf_op jit(solution)/shard_map/ppermute | solution.py:276
  48.9 17.7 %collective-permute-start.2 = (bf16[272,768]{1,0:T(8,128)(2,1)S(1)}, bf16[272,768]{1,0:T(8,128)(2,1)S(1)}, u32[]{:S(2)}, u32[]{:S(2)}) collective-permute-start(bf16[272,768]{1,0:T(8,128)(2,1)S(1)} %collective-permute-done.1.refs_2_), channel_id=1, source_target_pairs={{0,1},{1,0},{2,3},{3,2},{4,5},{5,4},{6,7},{7,6},{8,9},{9,8},{10,11... | collective-permute-start | bytes 1253384 | tf_op jit(solution)/shard_map/ppermute | solution.py:276
  48.9 17.7 %collective-permute-start.5 = (bf16[272,768]{1,0:T(8,128)(2,1)S(1)}, bf16[272,768]{1,0:T(8,128)(2,1)S(1)}, u32[]{:S(2)}, u32[]{:S(2)}) collective-permute-start(bf16[272,768]{1,0:T(8,128)(2,1)S(1)} %collective-permute-done.4.refs_6_), channel_id=1, source_target_pairs={{0,1},{1,0},{2,3},{3,2},{4,5},{5,4},{6,7},{7,6},{8,9},{9,8},{10,11... | collective-permute-start | bytes 1253384 | tf_op jit(solution)/shard_map/ppermute | solution.py:276
  57.9 8.8 %collective-permute-start.8 = (bf16[272,768]{1,0:T(8,128)(2,1)S(1)}, bf16[272,768]{1,0:T(8,128)(2,1)S(1)}, u32[]{:S(2)}, u32[]{:S(2)}) collective-permute-start(bf16[272,768]{1,0:T(8,128)(2,1)S(1)} %collective-permute-done.7.refs_10_), channel_id=1, source_target_pairs={{0,1},{1,0},{2,3},{3,2},{4,5},{5,4},{6,7},{7,6},{8,9},{9,8},{10,11... | collective-permute-start | bytes 1253384 | tf_op jit(solution)/shard_map/ppermute | solution.py:276
  92.7 148.4 %reduce-scatter.5.cloned.1.call-start = ((), (), s32[]{:S(2)}) async-start(), calls=%async_computation.3 | async-start | bytes 1216512 | tf_op jit(solution)/shard_map/reduce_scatter | solution.py:374
  95.6 3.4 collective-permute-start.21
  95.9 3.2 collective-permute-start.19
  97.2 11.8 %collective-permute-start.23 = (bf16[272,768]{1,0:T(8,128)(2,1)S(1)}, bf16[272,768]{1,0:T(8,128)(2,1)S(1)}, u32[]{:S(2)}, u32[]{:S(2)}) collective-permute-start(bf16[272,768]{1,0:T(8,128)(2,1)S(1)} %add_convert_fusion), channel_id=1, source_target_pairs={{0,2},{1,3},{2,0},{3,1},{4,6},{5,7},{6,4},{7,5},{8,10},{9,11},{10,... | collective-permute-start | bytes 1253384 | tf_op jit(solution)/shard_map/ppermute | solution.py:276
  126.0 222.3 %reduce-scatter.3.cloned.1.call-start = ((), (), s32[]{:S(2)}) async-start(), calls=%async_computation.2 | async-start | bytes 3649536 | tf_op jit(solution)/shard_map/reduce_scatter | solution.py:374
  128.4 3.7 %collective-permute-start.15 = (bf16[272,768]{1,0:T(8,128)(2,1)S(1)}, bf16[272,768]{1,0:T(8,128)(2,1)S(1)}, u32[]{:S(2)}, u32[]{:S(2)}) collective-permute-start(bf16[272,768]{1,0:T(8,128)(2,1)S(1)} %get-tuple-element.73), channel_id=1, source_target_pairs={{0,1},{1,0},{2,3},{3,2},{4,5},{5,4},{6,7},{7,6},{8,9},{9,8},{10,11... | collective-permute-start | bytes 1253384 | tf_op jit(solution)/shard_map/ppermute | solution.py:276
  128.9 3.2 collective-permute-start.13
  130.3 11.7 %collective-permute-start.17 = (bf16[272,768]{1,0:T(8,128)(2,1)S(1)}, bf16[272,768]{1,0:T(8,128)(2,1)S(1)}, u32[]{:S(2)}, u32[]{:S(2)}) collective-permute-start(bf16[272,768]{1,0:T(8,128)(2,1)S(1)} %add_convert_fusion.2), channel_id=1, source_target_pairs={{0,2},{1,3},{2,0},{3,1},{4,6},{5,7},{6,4},{7,5},{8,10},{9,11},{10,... | collective-permute-start | bytes 1253384 | tf_op jit(solution)/shard_map/ppermute | solution.py:276
  132.1 13.3 %collective-permute-start.12 = (bf16[272,768]{1,0:T(8,128)(2,1)S(1)}, bf16[272,768]{1,0:T(8,128)(2,1)S(1)}, u32[]{:S(2)}, u32[]{:S(2)}) collective-permute-start(bf16[272,768]{1,0:T(8,128)(2,1)S(1)} %get-tuple-element.76), channel_id=1, source_target_pairs={{0,1},{1,0},{2,3},{3,2},{4,5},{5,4},{6,7},{7,6},{8,9},{9,8},{10,11... | collective-permute-start | bytes 1253384 | tf_op jit(solution)/shard_map/ppermute | solution.py:276
  143.2 12.6 %collective-permute-start.14 = (bf16[272,768]{1,0:T(8,128)(2,1)S(1)}, bf16[272,768]{1,0:T(8,128)(2,1)S(1)}, u32[]{:S(2)}, u32[]{:S(2)}) collective-permute-start(bf16[272,768]{1,0:T(8,128)(2,1)S(1)} %get-tuple-element.72), channel_id=1, source_target_pairs={{0,2},{1,3},{2,0},{3,1},{4,6},{5,7},{6,4},{7,5},{8,10},{9,11},{10,... | collective-permute-start | bytes 1253384 | tf_op jit(solution)/shard_map/ppermute | solution.py:276
  145.0 11.9 %collective-permute-start.18 = (bf16[272,768]{1,0:T(8,128)(2,1)S(1)}, bf16[272,768]{1,0:T(8,128)(2,1)S(1)}, u32[]{:S(2)}, u32[]{:S(2)}) collective-permute-start(bf16[272,768]{1,0:T(8,128)(2,1)S(1)} %copy-done.3), channel_id=1, source_target_pairs={{0,1},{1,0},{2,3},{3,2},{4,5},{5,4},{6,7},{7,6},{8,9},{9,8},{10,11... | collective-permute-start | bytes 1253384 | tf_op jit(solution)/shard_map/ppermute | solution.py:276
  145.0 18.2 %collective-permute-start.20 = (bf16[272,768]{1,0:T(8,128)(2,1)S(1)}, bf16[272,768]{1,0:T(8,128)(2,1)S(1)}, u32[]{:S(2)}, u32[]{:S(2)}) collective-permute-start(bf16[272,768]{1,0:T(8,128)(2,1)S(1)} %copy-done.4), channel_id=1, source_target_pairs={{0,2},{1,3},{2,0},{3,1},{4,6},{5,7},{6,4},{7,5},{8,10},{9,11},{10,... | collective-permute-start | bytes 1253384 | tf_op jit(solution)/shard_map/ppermute | solution.py:276
  (24 other events, 269.8 us)
Sparse Core Ops, SparseCore 0:
  92.8 114.6 all-reduce.2
Sparse Core Ops, SparseCore 1:
  126.1 114.9 reduce-scatter.4
  246.4 101.9 reduce-scatter.2
